TPU v7x, 512 devices: a whole 4x8x8 slice. The times are simulated.
512 devices in a mesh: gx: 16 (over z, core), gy: 8 (over y), gz: 4 (over x).
Axes of the slice: x: 4, y: 8, z: 8, core: 2. Of those that a mesh axis runs over, the one named last changes fastest.
Arguments:
- start: float32 [4, 80, 256, 512], P(None, 'gx', 'gy', 'gz'), may hold values from -6 to 6
- rhs_block: float32 [4, 80, 256, 512], P(None, 'gx', 'gy', 'gz'), may hold values from -6 to 6
- coefficients: float32 [4, 80, 256, 512], P(None, 'gx', 'gy', 'gz'), may hold values from 0.5 to 2
Outputs:
- solution: float32 [4, 80, 256, 512], P(None, 'gx', 'gy', 'gz')
All inputs are finite; a program needn't handle non-finite values.
Results may differ from a plain program's by a relative error of at most 0.0003.
Values sent between devices are 32-bit elements; how exact they have to be, the bound alone decides.
A program may use at most 192 MiB of HBM per device.

v0:
```python
import jax
import jax.numpy as jnp
from jax import lax
from jax.sharding import PartitionSpec as P

S = 4
basis_shift = 8.75
basis_scale = 4.0


def padded(block, sides, width):
    for axis, dim in sides:
        count = lax.axis_size(axis)
        forward = [(i, i + 1) for i in range(count - 1)]
        backward = [(target, source) for source, target in forward]
        low = lax.ppermute(
            lax.slice_in_dim(block, block.shape[dim] - width, None, axis=dim), axis, forward
        )
        high = lax.ppermute(lax.slice_in_dim(block, 0, width, axis=dim), axis, backward)
        block = jnp.concatenate([low, block, high], axis=dim)
    return block


def stencil(field, coefs):
    center = field[:, 1:-1, 1:-1, 1:-1]
    result = coefs[0, 1:-1, 1:-1, 1:-1] * center
    result = result + coefs[1, 1:-1, 1:-1, 1:-1] * (center - field[:, 2:, 1:-1, 1:-1])
    result = result + coefs[1, :-2, 1:-1, 1:-1] * (center - field[:, :-2, 1:-1, 1:-1])
    result = result + coefs[2, 1:-1, 1:-1, 1:-1] * (center - field[:, 1:-1, 2:, 1:-1])
    result = result + coefs[2, 1:-1, :-2, 1:-1] * (center - field[:, 1:-1, :-2, 1:-1])
    result = result + coefs[3, 1:-1, 1:-1, 1:-1] * (center - field[:, 1:-1, 1:-1, 2:])
    result = result + coefs[3, 1:-1, 1:-1, :-2] * (center - field[:, 1:-1, 1:-1, :-2])
    return result


def reflect_rows(tall):
    count = tall.shape[0]
    entries = tall.shape[1]
    position = jnp.arange(entries)
    for j in range(count):
        column = jnp.where(position >= j, tall[j], 0.0)
        length = jnp.sqrt(jnp.sum(column * column))
        leading = tall[j, j]
        mirror = -jnp.where(leading >= 0, 1.0, -1.0) * length
        vector = column - mirror * (position == j).astype(jnp.float32)
        weight = jnp.sum(vector * vector)
        project = jnp.dot(tall, vector, precision=lax.Precision.HIGHEST) / weight
        tall = tall - 2.0 * project[:, None] * vector[None, :]
    factor = tall.T
    flip_sign = jnp.where(jnp.diagonal(factor) >= 0, 1.0, -1.0)
    return jnp.triu(factor * flip_sign[:, None])


def back_solve(triangle, values):
    count = triangle.shape[0]
    answer = [None] * count
    for i in reversed(range(count)):
        partial_sum = values[i]
        for j in range(i + 1, count):
            partial_sum = partial_sum - triangle[i, j] * answer[j]
        answer[i] = partial_sum / triangle[i, i]
    return jnp.stack(answer)


def least_squares(upper, nrhs):
    total = upper.shape[0]
    kept = total - nrhs
    rows = jnp.arange(total)[:, None]
    cols = jnp.arange(kept)[None, :]
    shifts = basis_shift * (rows == cols).astype(jnp.float32) + basis_scale * (
        rows == cols + nrhs
    ).astype(jnp.float32)
    mixed = jnp.dot(upper, shifts, precision=lax.Precision.HIGHEST)
    joined = jnp.concatenate([mixed, upper[:, :nrhs]], axis=1)
    reduced = reflect_rows(joined.T)
    return back_solve(reduced[:kept, :kept], reduced[:kept, kept:])


def local(start, rhs_block, coefficients):
    nrhs = start.shape[0]
    guess_ext, coef_ext = (
        padded(start, (("gx", 1), ("gy", 2), ("gz", 3)), 1),
        padded(coefficients, (("gx", 1), ("gy", 2), ("gz", 3)), 1),
    )
    blocks = [rhs_block - stencil(guess_ext, coef_ext)]
    for step in range(S):
        before = blocks[-1]
        widened = padded(before, (("gx", 1), ("gy", 2), ("gz", 3)), 1)
        blocks.append((stencil(widened, coef_ext) - basis_shift * before) / basis_scale)
    tall = jnp.stack(blocks).reshape(len(blocks) * nrhs, -1)
    local_gram = jnp.dot(tall, tall.T, precision=lax.Precision.HIGHEST)
    gram = lax.psum(local_gram, ("gx", "gy", "gz"))
    upper = jnp.linalg.cholesky(gram).T
    weights = least_squares(upper, nrhs)
    kept = tall.shape[0] - nrhs
    update = jnp.dot(weights.T, tall[:kept], precision=lax.Precision.HIGHEST)
    return start + update.reshape(start.shape)


def solution(mesh):
    placed = (P(None, "gx", "gy", "gz"), P(None, "gx", "gy", "gz"), P(None, "gx", "gy", "gz"))
    return jax.shard_map(
        local, mesh=mesh, in_specs=placed, out_specs=P(None, "gx", "gy", "gz"), check_vma=False
    )
```

profile of v0, /device:TPU:1, one launch (start us, length us, event | category | flops | bytes accessed | tf_op | source)
XLA Modules:
  0.0 541.6 jit_solution(3785583033890651326)
XLA Ops:
  0.9 5.5 %collective-permute-start.1 = (f32[4,1,32,128]{3,2,1,0:T(8,128)S(1)}, f32[4,1,32,128]{3,2,1,0:T(8,128)S(1)}, u32[]{:S(2)}, u32[]{:S(2)}) collective-permute-start(f32[4,1,32,128]{3,2,1,0:T(8,128)S(1)} %get-tuple-element.80), channel_id=1, source_target_pairs={{0,32},{32,64},{64,96},{96,128},{128,160},{160,192},{192,224},{224... | collective-permute-start | bytes 196616 | tf_op jit(solution)/shard_map/ppermute | solution.py:16
  6.5 4.7 collective-permute-start.4
  12.1 1.9 collective-permute-start.2
  14.0 2.4 collective-permute-start
  18.4 1.7 collective-permute-start.5
  20.1 1.3 collective-permute-start.8
  22.2 1.3 collective-permute-start.3
  24.1 5.2 collective-permute-start.6
  29.4 1.8 copy.480
  31.2 2.0 copy.479
  33.2 1.9 copy.481
  36.0 3.1 collective-permute-start.9
  41.9 1.3 copy.476
  43.2 1.3 collective-permute-start.7
  44.5 1.3 copy.483
  45.9 4.0 collective-permute-start.10
  50.8 2.4 fusion.42
  53.2 1.2 copy.482
  56.7 2.2 constant_dynamic-update-slice_fusion.9
  58.9 1.9 collective-permute-start.11
  60.8 5.3 collective-permute-start.12
  66.2 1.3 collective-permute-done.12
  67.5 1.3 collective-permute-start.13
  68.8 4.0 collective-permute-start.14
  74.9 1.3 copy.491
  76.2 1.3 collective-permute-start.15
  77.5 1.3 copy.493
  78.9 4.0 collective-permute-start.16
  85.1 1.6 constant_dynamic-update-slice_fusion.8
  88.8 1.9 collective-permute-start.17
  90.7 6.2 %collective-permute-start.18 = (f32[4,1,32,128]{3,2,1,0:T(8,128)S(1)}, f32[4,1,32,128]{3,2,1,0:T(8,128)S(1)}, u32[]{:S(2)}, u32[]{:S(2)}) collective-permute-start(f32[4,1,32,128]{3,2,1,0:T(8,128)S(1)} %get-tuple-element.70), channel_id=1, source_target_pairs={{0,32},{32,64},{64,96},{96,128},{128,160},{160,192},{192,224},{224... | collective-permute-start | bytes 196616 | tf_op jit(solution)/shard_map/ppermute | solution.py:16
  96.9 1.3 collective-permute-done.18
  98.3 1.3 collective-permute-start.19
  99.6 4.5 collective-permute-start.20
  105.6 1.3 collective-permute-start.21
  107.2 4.5 collective-permute-start.22
  113.3 1.2 constant_dynamic-update-slice_fusion.7
  115.3 1.9 collective-permute-start.23
  117.3 5.6 %collective-permute-start.24 = (f32[4,1,32,128]{3,2,1,0:T(8,128)S(1)}, f32[4,1,32,128]{3,2,1,0:T(8,128)S(1)}, u32[]{:S(2)}, u32[]{:S(2)}) collective-permute-start(f32[4,1,32,128]{3,2,1,0:T(8,128)S(1)} %get-tuple-element.68), channel_id=1, source_target_pairs={{0,32},{32,64},{64,96},{96,128},{128,160},{160,192},{192,224},{224... | collective-permute-start | bytes 196616 | tf_op jit(solution)/shard_map/ppermute | solution.py:16
  122.9 1.3 collective-permute-done.24
  124.2 1.3 collective-permute-start.25
  125.5 4.5 collective-permute-start.26
  131.5 1.3 collective-permute-start.27
  133.1 4.5 collective-permute-start.28
  139.3 1.9 collective-permute-start.29
  141.2 6.0 %collective-permute-start.30 = (f32[4,1,32,128]{3,2,1,0:T(8,128)S(1)}, f32[4,1,32,128]{3,2,1,0:T(8,128)S(1)}, u32[]{:S(2)}, u32[]{:S(2)}) collective-permute-start(f32[4,1,32,128]{3,2,1,0:T(8,128)S(1)} %get-tuple-element.62), channel_id=1, source_target_pairs={{0,32},{32,64},{64,96},{96,128},{128,160},{160,192},{192,224},{224... | collective-permute-start | bytes 196616 | tf_op jit(solution)/shard_map/ppermute | solution.py:16
  147.3 1.3 collective-permute-done.30
  148.6 1.3 collective-permute-start.31
  149.9 5.5 %collective-permute-start.32 = (f32[4,7,1,128]{3,0,2,1:T(4,128)S(1)}, f32[4,7,1,128]{3,0,2,1:T(4,128)S(1)}, u32[]{:S(2)}, u32[]{:S(2)}) collective-permute-start(f32[4,7,1,128]{3,0,2,1:T(4,128)S(1)} %copy.517), channel_id=1, source_target_pairs={{0,4},{4,8},{8,12},{12,16},{16,20},{20,24},{24,28},{1,5},{5,9},{9,... | collective-permute-start | bytes 43016 | tf_op jit(solution)/shard_map/ppermute | solution.py:16
  156.8 1.3 collective-permute-start.33
  159.0 5.1 collective-permute-start.34
  164.1 1.2 pad_maximum_fusion
  165.3 1.3 slice.1287
  166.6 1.6 copy.552
  169.3 1.8 copy.524
  171.2 2.2 fusion.49
  173.5 1.7 reshape.530
  175.2 2.1 fusion.311
  177.3 116.5 %psum.7 = f32[20,20]{0,1:T(8,128)S(1)} all-reduce(f32[20,20]{0,1:T(8,128)S(1)} %fusion.311), channel_id=1, replica_groups=mesh['gx'=16,'gy'=8,'gz'=4] {'gx','gy','gz'}, use_global_device_ids=true, to_apply=%region_0.0 | all-reduce | flops 400 | bytes 3200 | tf_op jit(solution)/shard_map/psum | solution.py:92
  293.9 1.8 cholesky.19
  395.1 65.5 %subtract_divide_fusion = (f32[1,4]{1,0:T(1,128)S(1)}, f32[1,4]{1,0:T(1,128)S(1)}, f32[1,4]{1,0:T(1,128)S(1)}, f32[1,4]{1,0:T(1,128)S(1)}, f32[1,4]{1,0:T(1,128)...) fusion(f32[20,20]{1,0:T(8,128)S(1)} %multiply_select_fusion, ...), kind=kLoop, calls=%fused_computation.602 | loop fusion | flops 784 | bytes 884 | tf_op jit(solution)/shard_map/div | solution.py:61
  461.0 57.8 %fusion.191 = (f32[4]{0:T(128)S(1)}, f32[4]{0:T(128)S(1)}, f32[4]{0:T(128)S(1)}, f32[4]{0:T(128)S(1)}, f32[4]{0:T(128)S(1)}, /*index=5*/f32[4]{0:T(128)S(1)}, f3...) fusion(f32[20,20]{1,0:T(8,128)S(1)} %multiply_select_fusion, f32[1,4]{1,0:T(1,128)S(1)} %get-tuple-element.16, ...), kind=kLoop, calls=%fused_computation.504 | loop fusion | flops 704 | bytes 756 | tf_op jit(solution)/shard_map/div | solution.py:61
  518.8 19.3 %fusion.244 = (f32[1,4]{1,0:T(1,128)S(1)}, f32[4]{0:T(128)S(1)}) fusion(f32[1,4]{1,0:T(1,128)S(1)} %get-tuple-element.19, f32[1,4]{1,0:T(1,128)S(1)} %get-tuple-element.18, f32[1,4]{1,0:T(1,128)S(1)} %get-tuple-element.17, f32[1,4]{1,0:T(1,128)S(1)} %get-tuple-element.16, f32[4]{0:T(128)S(1)} %get-tuple-element.31, f32[4]{0:T(128)S(1)} %get-tuple-element.30, ...), kind=kLoop, calls=%fused_computation.656 | loop fusion | flops 240 | bytes 412 | tf_op jit(solution)/shard_map/stack | solution.py:62
  539.3 1.4 fusion
  (338 shorter events, 102.8 us)
Async XLA Ops:
  0.0 21.4 %copy-start.1 = (f32[4,5,32,128]{3,2,1,0:T(8,128)S(1)}, f32[4,5,32,128]{3,2,1,0:T(8,128)}, u32[]{:S(2)}) copy-start(f32[4,5,32,128]{3,2,1,0:T(8,128)} %param.3) | copy-start | bytes 983044
  0.9 28.4 %copy-start = (f32[4,5,32,128]{3,2,1,0:T(8,128)S(1)}, f32[4,5,32,128]{3,2,1,0:T(8,128)}, u32[]{:S(2)}) copy-start(f32[4,5,32,128]{3,2,1,0:T(8,128)} %param.5) | copy-start | bytes 983044
  0.9 15.5 %collective-permute-start.1 = (f32[4,1,32,128]{3,2,1,0:T(8,128)S(1)}, f32[4,1,32,128]{3,2,1,0:T(8,128)S(1)}, u32[]{:S(2)}, u32[]{:S(2)}) collective-permute-start(f32[4,1,32,128]{3,2,1,0:T(8,128)S(1)} %get-tuple-element.80), channel_id=1, source_target_pairs={{0,32},{32,64},{64,96},{96,128},{128,160},{160,192},{192,224},{224... | collective-permute-start | bytes 196616 | tf_op jit(solution)/shard_map/ppermute | solution.py:16
  6.5 11.0 %collective-permute-start.4 = (f32[4,1,32,128]{3,2,1,0:T(8,128)S(1)}, f32[4,1,32,128]{3,2,1,0:T(8,128)S(1)}, u32[]{:S(2)}, u32[]{:S(2)}) collective-permute-start(f32[4,1,32,128]{3,2,1,0:T(8,128)S(1)} %get-tuple-element.79), channel_id=1, source_target_pairs={{32,0},{64,32},{96,64},{128,96},{160,128},{192,160},{224,192},{256... | collective-permute-start | bytes 196616 | tf_op jit(solution)/shard_map/ppermute | solution.py:19
  12.1 9.3 %collective-permute-start.2 = (f32[4,1,32,128]{3,2,1,0:T(8,128)S(1)}, f32[4,1,32,128]{3,2,1,0:T(8,128)S(1)}, u32[]{:S(2)}, u32[]{:S(2)}) collective-permute-start(f32[4,1,32,128]{3,2,1,0:T(8,128)S(1)} %get-tuple-element.82), channel_id=1, source_target_pairs={{0,32},{32,64},{64,96},{96,128},{128,160},{160,192},{192,224},{224... | collective-permute-start | bytes 196616 | tf_op jit(solution)/shard_map/ppermute | solution.py:16
  14.0 7.5 %collective-permute-start = (f32[4,1,32,128]{3,2,1,0:T(8,128)S(1)}, f32[4,1,32,128]{3,2,1,0:T(8,128)S(1)}, u32[]{:S(2)}, u32[]{:S(2)}) collective-permute-start(f32[4,1,32,128]{3,2,1,0:T(8,128)S(1)} %get-tuple-element.81), channel_id=1, source_target_pairs={{32,0},{64,32},{96,64},{128,96},{160,128},{192,160},{224,192},{256... | collective-permute-start | bytes 196616 | tf_op jit(solution)/shard_map/ppermute | solution.py:19
  17.5 3.9 copy-start.20
  17.7 11.6 %copy-start.19 = (f32[4,7,32,128]{3,1,2,0:T(8,128)}, f32[4,7,32,128]{3,1,2,0:T(8,128)S(1)}, u32[]{:S(2)}) copy-start(f32[4,7,32,128]{3,1,2,0:T(8,128)S(1)} %copy.469) | copy-start | bytes 1376260
  18.4 12.8 %collective-permute-start.5 = (f32[4,7,1,128]{3,1,2,0:T(8,128)}, f32[4,7,1,128]{3,1,2,0:T(8,128)S(1)}, u32[]{:S(2)}, u32[]{:S(2)}) collective-permute-start(f32[4,7,1,128]{3,1,2,0:T(8,128)} %get-tuple-element.50), channel_id=1, source_target_pairs={{0,4},{4,8},{8,12},{12,16},{16,20},{20,24},{24,28},{1,5},{5,9},{9,... | collective-permute-start | bytes 43016 | tf_op jit(solution)/shard_map/ppermute | solution.py:16
  20.1 13.1 %collective-permute-start.8 = (f32[4,7,1,128]{3,1,2,0:T(8,128)}, f32[4,7,1,128]{3,1,2,0:T(8,128)S(1)}, u32[]{:S(2)}, u32[]{:S(2)}) collective-permute-start(f32[4,7,1,128]{3,1,2,0:T(8,128)} %get-tuple-element.51), channel_id=1, source_target_pairs={{4,0},{8,4},{12,8},{16,12},{20,16},{24,20},{28,24},{5,1},{9,5},{13... | collective-permute-start | bytes 43016 | tf_op jit(solution)/shard_map/ppermute | solution.py:19
  21.5 2.7 copy-start.24
  21.5 2.6 copy-start.17
  22.2 16.9 %collective-permute-start.3 = (f32[4,7,1,128]{3,0,2,1:T(4,128)}, f32[4,7,1,128]{3,0,2,1:T(4,128)}, u32[]{:S(2)}, u32[]{:S(2)}) collective-permute-start(f32[4,7,1,128]{3,0,2,1:T(4,128)} %copy.550), channel_id=1, source_target_pairs={{4,0},{8,4},{12,8},{16,12},{20,16},{24,20},{28,24},{5,1},{9,5},{13... | collective-permute-start | bytes 43016 | tf_op jit(solution)/shard_map/ppermute | solution.py:19
  24.1 15.8 %collective-permute-start.6 = (f32[4,7,1,128]{3,0,2,1:T(4,128)}, f32[4,7,1,128]{3,0,2,1:T(4,128)}, u32[]{:S(2)}, u32[]{:S(2)}) collective-permute-start(f32[4,7,1,128]{3,0,2,1:T(4,128)} %copy.551), channel_id=1, source_target_pairs={{0,4},{4,8},{8,12},{12,16},{16,20},{20,24},{24,28},{1,5},{5,9},{9,... | collective-permute-start | bytes 43016 | tf_op jit(solution)/shard_map/ppermute | solution.py:16
  29.4 55.7 %copy-start.5 = (f32[5,32,128]{2,1,0:T(8,128)}, f32[5,32,128]{2,1,0:T(8,128)S(1)}, u32[]{:S(2)}) copy-start(f32[5,32,128]{2,1,0:T(8,128)S(1)} %get-tuple-element.77) | copy-start | bytes 245764
  29.4 55.7 %copy-start.8 = (f32[5,32,128]{2,1,0:T(8,128)}, f32[5,32,128]{2,1,0:T(8,128)S(1)}, u32[]{:S(2)}) copy-start(f32[5,32,128]{2,1,0:T(8,128)S(1)} %get-tuple-element.78) | copy-start | bytes 245764
  29.4 109.4 %copy-start.3 = (f32[5,32,128]{2,1,0:T(8,128)}, f32[5,32,128]{2,1,0:T(8,128)S(1)}, u32[]{:S(2)}) copy-start(f32[5,32,128]{2,1,0:T(8,128)S(1)} %get-tuple-element.76) | copy-start | bytes 245764
  35.2 5.5 %copy-start.18 = (f32[4,7,32,128]{3,2,1,0:T(8,128)S(1)}, f32[4,7,32,128]{3,2,1,0:T(8,128)}, u32[]{:S(2)}) copy-start(f32[4,7,32,128]{3,2,1,0:T(8,128)} %copy-done.17) | copy-start | bytes 1376260
  36.0 14.8 %collective-permute-start.9 = (f32[4,7,34,1]{2,1,3,0:T(8,128)S(1)}, f32[4,7,34,1]{2,1,3,0:T(8,128)S(1)}, u32[]{:S(2)}, u32[]{:S(2)}) collective-permute-start(f32[4,7,34,1]{2,1,3,0:T(8,128)S(1)} %pad_maximum_fusion.93), channel_id=1, source_target_pairs={{0,1},{1,2},{2,3},{4,5},{5,6},{6,7},{8,9},{9,10},{10,11},{12,13},{... | collective-permute-start | bytes 11432 | tf_op jit(solution)/shard_map/ppermute | solution.py:16
  43.2 11.2 %collective-permute-start.7 = (f32[4,7,34,1]{2,0,3,1:T(4,128)S(1)}, f32[4,7,34,1]{2,0,3,1:T(4,128)S(1)}, u32[]{:S(2)}, u32[]{:S(2)}) collective-permute-start(f32[4,7,34,1]{2,0,3,1:T(4,128)S(1)} %copy.476), channel_id=1, source_target_pairs={{1,0},{2,1},{3,2},{5,4},{6,5},{7,6},{9,8},{10,9},{11,10},{13,12},{... | collective-permute-start | bytes 11432 | tf_op jit(solution)/shard_map/ppermute | solution.py:19
  45.9 9.7 %collective-permute-start.10 = (f32[4,7,34,1]{2,0,3,1:T(4,128)S(1)}, f32[4,7,34,1]{2,0,3,1:T(4,128)S(1)}, u32[]{:S(2)}, u32[]{:S(2)}) collective-permute-start(f32[4,7,34,1]{2,0,3,1:T(4,128)S(1)} %copy.483), channel_id=1, source_target_pairs={{0,1},{1,2},{2,3},{4,5},{5,6},{6,7},{8,9},{9,10},{10,11},{12,13},{... | collective-permute-start | bytes 11432 | tf_op jit(solution)/shard_map/ppermute | solution.py:16
  50.8 34.3 %copy-start.11 = (f32[5,32,128]{2,1,0:T(8,128)}, f32[5,32,128]{2,1,0:T(8,128)S(1)}, u32[]{:S(2)}) copy-start(f32[5,32,128]{2,1,0:T(8,128)S(1)} %copy.471) | copy-start | bytes 245764
  53.2 3.5 copy-start.23
  53.2 3.5 copy-start.25
  54.4 84.4 %copy-start.14 = (f32[5,32,128]{2,1,0:T(8,128)}, f32[5,32,128]{2,1,0:T(8,128)S(1)}, u32[]{:S(2)}) copy-start(f32[5,32,128]{2,1,0:T(8,128)S(1)} %copy.482) | copy-start | bytes 245764
  58.9 7.3 %collective-permute-start.11 = (f32[4,1,32,128]{3,2,1,0:T(8,128)S(1)}, f32[4,1,32,128]{3,2,1,0:T(8,128)S(1)}, u32[]{:S(2)}, u32[]{:S(2)}) collective-permute-start(f32[4,1,32,128]{3,2,1,0:T(8,128)S(1)} %get-tuple-element.73), channel_id=1, source_target_pairs={{32,0},{64,32},{96,64},{128,96},{160,128},{192,160},{224,192},{256... | collective-permute-start | bytes 196616 | tf_op jit(solution)/shard_map/ppermute | solution.py:19
  60.8 6.6 %collective-permute-start.12 = (f32[4,1,32,128]{3,2,1,0:T(8,128)S(1)}, f32[4,1,32,128]{3,2,1,0:T(8,128)S(1)}, u32[]{:S(2)}, u32[]{:S(2)}) collective-permute-start(f32[4,1,32,128]{3,2,1,0:T(8,128)S(1)} %get-tuple-element.72), channel_id=1, source_target_pairs={{0,32},{32,64},{64,96},{96,128},{128,160},{160,192},{192,224},{224... | collective-permute-start | bytes 196616 | tf_op jit(solution)/shard_map/ppermute | solution.py:16
  67.5 5.3 collective-permute-start.13
  68.8 4.8 collective-permute-start.14
  76.2 6.6 %collective-permute-start.15 = (f32[4,7,34,1]{2,0,3,1:T(4,128)S(1)}, f32[4,7,34,1]{2,0,3,1:T(4,128)S(1)}, u32[]{:S(2)}, u32[]{:S(2)}) collective-permute-start(f32[4,7,34,1]{2,0,3,1:T(4,128)S(1)} %copy.491), channel_id=1, source_target_pairs={{1,0},{2,1},{3,2},{5,4},{6,5},{7,6},{9,8},{10,9},{11,10},{13,12},{... | collective-permute-start | bytes 11432 | tf_op jit(solution)/shard_map/ppermute | solution.py:19
  78.9 5.1 collective-permute-start.16
  86.8 1.2 copy-start.16
  88.8 8.2 %collective-permute-start.17 = (f32[4,1,32,128]{3,2,1,0:T(8,128)S(1)}, f32[4,1,32,128]{3,2,1,0:T(8,128)S(1)}, u32[]{:S(2)}, u32[]{:S(2)}) collective-permute-start(f32[4,1,32,128]{3,2,1,0:T(8,128)S(1)} %get-tuple-element.71), channel_id=1, source_target_pairs={{32,0},{64,32},{96,64},{128,96},{160,128},{192,160},{224,192},{256... | collective-permute-start | bytes 196616 | tf_op jit(solution)/shard_map/ppermute | solution.py:19
  90.7 7.5 %collective-permute-start.18 = (f32[4,1,32,128]{3,2,1,0:T(8,128)S(1)}, f32[4,1,32,128]{3,2,1,0:T(8,128)S(1)}, u32[]{:S(2)}, u32[]{:S(2)}) collective-permute-start(f32[4,1,32,128]{3,2,1,0:T(8,128)S(1)} %get-tuple-element.70), channel_id=1, source_target_pairs={{0,32},{32,64},{64,96},{96,128},{128,160},{160,192},{192,224},{224... | collective-permute-start | bytes 196616 | tf_op jit(solution)/shard_map/ppermute | solution.py:16
  98.3 5.9 %collective-permute-start.19 = (f32[4,7,1,128]{3,0,2,1:T(4,128)S(1)}, f32[4,7,1,128]{3,0,2,1:T(4,128)S(1)}, u32[]{:S(2)}, u32[]{:S(2)}) collective-permute-start(f32[4,7,1,128]{3,0,2,1:T(4,128)S(1)} %copy.495), channel_id=1, source_target_pairs={{4,0},{8,4},{12,8},{16,12},{20,16},{24,20},{28,24},{5,1},{9,5},{13... | collective-permute-start | bytes 43016 | tf_op jit(solution)/shard_map/ppermute | solution.py:19
  99.6 5.4 collective-permute-start.20
  105.3 8.0 %copy-start.6 = (f32[5,32,128]{2,1,0:T(8,128)S(1)}, f32[5,32,128]{2,1,0:T(8,128)}, u32[]{:S(2)}) copy-start(f32[5,32,128]{2,1,0:T(8,128)} %copy-done.5) | copy-start | bytes 245764
  105.3 8.0 %copy-start.9 = (f32[5,32,128]{2,1,0:T(8,128)S(1)}, f32[5,32,128]{2,1,0:T(8,128)}, u32[]{:S(2)}) copy-start(f32[5,32,128]{2,1,0:T(8,128)} %copy-done.8) | copy-start | bytes 245764
  105.3 8.0 %copy-start.12 = (f32[5,32,128]{2,1,0:T(8,128)S(1)}, f32[5,32,128]{2,1,0:T(8,128)}, u32[]{:S(2)}) copy-start(f32[5,32,128]{2,1,0:T(8,128)} %copy-done.11) | copy-start | bytes 245764
  105.6 7.0 %collective-permute-start.21 = (f32[4,7,34,1]{2,0,3,1:T(4,128)S(1)}, f32[4,7,34,1]{2,0,3,1:T(4,128)S(1)}, u32[]{:S(2)}, u32[]{:S(2)}) collective-permute-start(f32[4,7,34,1]{2,0,3,1:T(4,128)S(1)} %copy.501), channel_id=1, source_target_pairs={{1,0},{2,1},{3,2},{5,4},{6,5},{7,6},{9,8},{10,9},{11,10},{13,12},{... | collective-permute-start | bytes 11432 | tf_op jit(solution)/shard_map/ppermute | solution.py:19
  107.2 5.8 %collective-permute-start.22 = (f32[4,7,34,1]{2,0,3,1:T(4,128)S(1)}, f32[4,7,34,1]{2,0,3,1:T(4,128)S(1)}, u32[]{:S(2)}, u32[]{:S(2)}) collective-permute-start(f32[4,7,34,1]{2,0,3,1:T(4,128)S(1)} %copy.503), channel_id=1, source_target_pairs={{0,1},{1,2},{2,3},{4,5},{5,6},{6,7},{8,9},{9,10},{10,11},{12,13},{... | collective-permute-start | bytes 11432 | tf_op jit(solution)/shard_map/ppermute | solution.py:16
  112.6 26.2 %copy-start.21 = (f32[5,32,128]{2,1,0:T(8,128)}, f32[5,32,128]{2,1,0:T(8,128)S(1)}, u32[]{:S(2)}) copy-start(f32[5,32,128]{2,1,0:T(8,128)S(1)} %broadcast_multiply_fusion.3) | copy-start | bytes 245764
  115.3 7.5 %collective-permute-start.23 = (f32[4,1,32,128]{3,2,1,0:T(8,128)S(1)}, f32[4,1,32,128]{3,2,1,0:T(8,128)S(1)}, u32[]{:S(2)}, u32[]{:S(2)}) collective-permute-start(f32[4,1,32,128]{3,2,1,0:T(8,128)S(1)} %get-tuple-element.69), channel_id=1, source_target_pairs={{32,0},{64,32},{96,64},{128,96},{160,128},{192,160},{224,192},{256... | collective-permute-start | bytes 196616 | tf_op jit(solution)/shard_map/ppermute | solution.py:19
  117.3 6.9 %collective-permute-start.24 = (f32[4,1,32,128]{3,2,1,0:T(8,128)S(1)}, f32[4,1,32,128]{3,2,1,0:T(8,128)S(1)}, u32[]{:S(2)}, u32[]{:S(2)}) collective-permute-start(f32[4,1,32,128]{3,2,1,0:T(8,128)S(1)} %get-tuple-element.68), channel_id=1, source_target_pairs={{0,32},{32,64},{64,96},{96,128},{128,160},{160,192},{192,224},{224... | collective-permute-start | bytes 196616 | tf_op jit(solution)/shard_map/ppermute | solution.py:16
  124.2 5.9 %collective-permute-start.25 = (f32[4,7,1,128]{3,0,2,1:T(4,128)S(1)}, f32[4,7,1,128]{3,0,2,1:T(4,128)S(1)}, u32[]{:S(2)}, u32[]{:S(2)}) collective-permute-start(f32[4,7,1,128]{3,0,2,1:T(4,128)S(1)} %copy.505), channel_id=1, source_target_pairs={{4,0},{8,4},{12,8},{16,12},{20,16},{24,20},{28,24},{5,1},{9,5},{13... | collective-permute-start | bytes 43016 | tf_op jit(solution)/shard_map/ppermute | solution.py:19
  125.5 5.4 collective-permute-start.26
  131.5 6.1 %collective-permute-start.27 = (f32[4,7,34,1]{2,0,3,1:T(4,128)S(1)}, f32[4,7,34,1]{2,0,3,1:T(4,128)S(1)}, u32[]{:S(2)}, u32[]{:S(2)}) collective-permute-start(f32[4,7,34,1]{2,0,3,1:T(4,128)S(1)} %copy.511), channel_id=1, source_target_pairs={{1,0},{2,1},{3,2},{5,4},{6,5},{7,6},{9,8},{10,9},{11,10},{13,12},{... | collective-permute-start | bytes 11432 | tf_op jit(solution)/shard_map/ppermute | solution.py:19
  133.1 5.4 collective-permute-start.28
  139.3 7.9 %collective-permute-start.29 = (f32[4,1,32,128]{3,2,1,0:T(8,128)S(1)}, f32[4,1,32,128]{3,2,1,0:T(8,128)S(1)}, u32[]{:S(2)}, u32[]{:S(2)}) collective-permute-start(f32[4,1,32,128]{3,2,1,0:T(8,128)S(1)} %get-tuple-element.63), channel_id=1, source_target_pairs={{32,0},{64,32},{96,64},{128,96},{160,128},{192,160},{224,192},{256... | collective-permute-start | bytes 196616 | tf_op jit(solution)/shard_map/ppermute | solution.py:19
  141.2 7.3 %collective-permute-start.30 = (f32[4,1,32,128]{3,2,1,0:T(8,128)S(1)}, f32[4,1,32,128]{3,2,1,0:T(8,128)S(1)}, u32[]{:S(2)}, u32[]{:S(2)}) collective-permute-start(f32[4,1,32,128]{3,2,1,0:T(8,128)S(1)} %get-tuple-element.62), channel_id=1, source_target_pairs={{0,32},{32,64},{64,96},{96,128},{128,160},{160,192},{192,224},{224... | collective-permute-start | bytes 196616 | tf_op jit(solution)/shard_map/ppermute | solution.py:16
  148.6 7.5 %collective-permute-start.31 = (f32[4,7,1,128]{3,0,2,1:T(4,128)S(1)}, f32[4,7,1,128]{3,0,2,1:T(4,128)S(1)}, u32[]{:S(2)}, u32[]{:S(2)}) collective-permute-start(f32[4,7,1,128]{3,0,2,1:T(4,128)S(1)} %copy.515), channel_id=1, source_target_pairs={{4,0},{8,4},{12,8},{16,12},{20,16},{24,20},{28,24},{5,1},{9,5},{13... | collective-permute-start | bytes 43016 | tf_op jit(solution)/shard_map/ppermute | solution.py:19
  149.9 6.3 %collective-permute-start.32 = (f32[4,7,1,128]{3,0,2,1:T(4,128)S(1)}, f32[4,7,1,128]{3,0,2,1:T(4,128)S(1)}, u32[]{:S(2)}, u32[]{:S(2)}) collective-permute-start(f32[4,7,1,128]{3,0,2,1:T(4,128)S(1)} %copy.517), channel_id=1, source_target_pairs={{0,4},{4,8},{8,12},{12,16},{16,20},{20,24},{24,28},{1,5},{5,9},{9,... | collective-permute-start | bytes 43016 | tf_op jit(solution)/shard_map/ppermute | solution.py:16
  156.8 11.5 %collective-permute-start.33 = (f32[4,7,34,1]{2,0,3,1:T(4,128)S(1)}, f32[4,7,34,1]{2,0,3,1:T(4,128)}, u32[]{:S(2)}, u32[]{:S(2)}) collective-permute-start(f32[4,7,34,1]{2,0,3,1:T(4,128)S(1)} %copy.521), channel_id=1, source_target_pairs={{1,0},{2,1},{3,2},{5,4},{6,5},{7,6},{9,8},{10,9},{11,10},{13,12},{... | collective-permute-start | bytes 11432 | tf_op jit(solution)/shard_map/ppermute | solution.py:19
  159.0 10.4 %collective-permute-start.34 = (f32[4,7,34,1]{2,0,3,1:T(4,128)}, f32[4,7,34,1]{2,0,3,1:T(4,128)}, u32[]{:S(2)}, u32[]{:S(2)}) collective-permute-start(f32[4,7,34,1]{2,0,3,1:T(4,128)} %copy.523), channel_id=1, source_target_pairs={{0,1},{1,2},{2,3},{4,5},{5,6},{6,7},{8,9},{9,10},{10,11},{12,13},{... | collective-permute-start | bytes 11432 | tf_op jit(solution)/shard_map/ppermute | solution.py:16
  166.6 4.5 copy-start.4
  166.6 4.6 copy-start.7
  166.6 4.6 copy-start.10
  166.6 4.6 copy-start.13
  166.6 4.6 copy-start.15
  166.6 4.6 copy-start.22
  384.5 156.3 %copy-start.2 = (f32[4,5,32,128]{3,2,1,0:T(8,128)S(1)}, f32[4,5,32,128]{3,2,1,0:T(8,128)}, u32[]{:S(2)}) copy-start(f32[4,5,32,128]{3,2,1,0:T(8,128)} %param.3) | copy-start | bytes 983044
where the time goes:
time: 546 us; the launch traced here: 542 us
  other arithmetic  195 us (36%)
  blocking collectives  116 us (21%)
  starting transfers between devices  110 us (20%)
  local copies, waits for them, and re-layouts  62.4 us (11%)
  between operations  29.3 us (5%)
  matrix products  20.1 us (4%)
  waiting for transfers between devices  8.15 us (1%)
    div x2, other arithmetic, back_solve(): answer[i] = partial_sum / triangle[i, i]  123 us
    psum x1, blocking collectives, local(): gram = lax.psum(local_gram, ('gx', 'gy', 'gz'))  116 us
    ppermute x18, starting transfers between devices, padded(): lax.ppermute(lax.slice_in_dim(block, block.shape[dim] - width, None, axis...  81.2 us
    ppermute x17, starting transfers between devices, padded(): lax.ppermute(lax.slice_in_dim(block, 0, width, axis=dim), axis, backward)  28.9 us
    another operation x1, other arithmetic, back_solve(): return jnp.stack(answer)  19.3 us
    dot_general x20, matrix products, reflect_rows(): project = jnp.dot(tall, vector, precision=lax.Precision.HIGHEST) / weight  15.7 us
    reduce_sum x20, other arithmetic, reflect_rows(): length = jnp.sqrt(jnp.sum(column * column))  13.6 us
    reduce_sum x20, other arithmetic, reflect_rows(): weight = jnp.sum(vector * vector)  12 us
  transfers between devices with their start and end apart: 35, of which 8 were waited for; matrix products, arithmetic and copies ran while one was open for 6% of the time, Pallas kernels for 0%

commit v1 on v0

--- a/solution.py
+++ b/solution.py
@@ -2,6 +2,7 @@
 import jax.numpy as jnp
 from jax import lax
 from jax.sharding import PartitionSpec as P
+from jax.lax import psum
 
 S = 4
 basis_shift = 8.75
@@ -89,7 +90,9 @@
         blocks.append((stencil(widened, coef_ext) - basis_shift * before) / basis_scale)
     tall = jnp.stack(blocks).reshape(len(blocks) * nrhs, -1)
     local_gram = jnp.dot(tall, tall.T, precision=lax.Precision.HIGHEST)
-    gram = lax.psum(local_gram, ("gx", "gy", "gz"))
+    gram = local_gram
+    for t in (("gy", "gz"), "gx"):
+        gram = psum(gram, t)
     upper = jnp.linalg.cholesky(gram).T
     weights = least_squares(upper, nrhs)
     kept = tall.shape[0] - nrhs

time: 546 us -> 633 us (1.16)
  blocking collectives: 116 us -> 201 us
    psum x1 -> x2, blocking collectives: 116 us -> 201 us  [local(): gram = psum(gram, t)]
  transfers between devices with their start and end apart: 35 -> 35, of which waited for: 8 -> 8; matrix products, arithmetic and copies ran while one was open for 6% -> 5% of each run, Pallas kernels for 0% -> 0%
where the time goes in v1:
time: 633 us; the launch traced here: 626 us
  blocking collectives  201 us (32%)
  other arithmetic  195 us (31%)
  starting transfers between devices  110 us (17%)
  local copies, waits for them, and re-layouts  62.4 us (10%)
  between operations  29.3 us (5%)
  matrix products  20.1 us (3%)
  waiting for transfers between devices  8.15 us (1%)
    psum x2, blocking collectives, local(): gram = psum(gram, t)  201 us
    div x2, other arithmetic, back_solve(): answer[i] = partial_sum / triangle[i, i]  123 us
    ppermute x18, starting transfers between devices, padded(): lax.ppermute(lax.slice_in_dim(block, block.shape[dim] - width, None, axis...  81.2 us
    ppermute x17, starting transfers between devices, padded(): lax.ppermute(lax.slice_in_dim(block, 0, width, axis=dim), axis, backward)  28.9 us
    another operation x1, other arithmetic, back_solve(): return jnp.stack(answer)  19.3 us
    dot_general x20, matrix products, reflect_rows(): project = jnp.dot(tall, vector, precision=lax.Precision.HIGHEST) / weight  15.7 us
    reduce_sum x20, other arithmetic, reflect_rows(): length = jnp.sqrt(jnp.sum(column * column))  13.6 us
  transfers between devices with their start and end apart: 35, of which 8 were waited for; matrix products, arithmetic and copies ran while one was open for 5% of the time, Pallas kernels for 0%

profile of v1, /device:TPU:1, one launch (start us, length us, event | category | flops | bytes accessed | tf_op | source)
XLA Modules:
  0.0 625.6 jit_solution(4169096291923980434)
XLA Ops:
  0.9 5.5 collective-permute-start.1
  6.5 4.7 collective-permute-start.4
  12.1 1.9 collective-permute-start.2
  14.0 2.4 collective-permute-start
  18.4 1.7 collective-permute-start.5
  20.1 1.3 collective-permute-start.8
  22.2 1.3 collective-permute-start.3
  24.1 5.2 collective-permute-start.6
  29.4 1.8 copy.480
  31.2 2.0 copy.479
  33.2 1.9 copy.481
  36.0 3.1 collective-permute-start.9
  41.9 1.3 copy.476
  43.2 1.3 collective-permute-start.7
  44.5 1.3 copy.483
  45.9 4.0 collective-permute-start.10
  50.8 2.4 fusion.42
  53.2 1.2 copy.482
  56.7 2.2 constant_dynamic-update-slice_fusion.9
  58.9 1.9 collective-permute-start.11
  60.8 5.3 collective-permute-start.12
  66.2 1.3 collective-permute-done.12
  67.5 1.3 collective-permute-start.13
  68.8 4.0 collective-permute-start.14
  74.9 1.3 copy.491
  76.2 1.3 collective-permute-start.15
  77.5 1.3 copy.493
  78.9 4.0 collective-permute-start.16
  85.1 1.6 constant_dynamic-update-slice_fusion.8
  88.8 1.9 collective-permute-start.17
  90.7 6.2 collective-permute-start.18
  96.9 1.3 collective-permute-done.18
  98.3 1.3 collective-permute-start.19
  99.6 4.5 collective-permute-start.20
  105.6 1.3 collective-permute-start.21
  107.2 4.5 collective-permute-start.22
  113.3 1.2 constant_dynamic-update-slice_fusion.7
  115.3 1.9 collective-permute-start.23
  117.3 5.6 collective-permute-start.24
  122.9 1.3 collective-permute-done.24
  124.2 1.3 collective-permute-start.25
  125.5 4.5 collective-permute-start.26
  131.5 1.3 collective-permute-start.27
  133.1 4.5 collective-permute-start.28
  139.3 1.9 collective-permute-start.29
  141.2 6.0 collective-permute-start.30
  147.3 1.3 collective-permute-done.30
  148.6 1.3 collective-permute-start.31
  149.9 5.5 collective-permute-start.32
  156.8 1.3 collective-permute-start.33
  159.0 5.1 collective-permute-start.34
  165.3 1.3 slice.1287
  166.6 1.6 copy.552
  169.3 1.8 copy.524
  171.2 2.2 fusion.49
  173.5 1.7 reshape.530
  175.2 2.1 fusion.311
  177.3 121.5 %psum.14 = f32[20,20]{0,1:T(8,128)S(1)} all-reduce(f32[20,20]{0,1:T(8,128)S(1)} %fusion.311), channel_id=1, replica_groups=mesh['gx'=16,'gy'=8,'gz'=4] {'gy','gz'}, use_global_device_ids=true, to_apply=%region_0.0 | all-reduce | flops 400 | bytes 3200 | tf_op jit(solution)/shard_map/psum | solution.py:95
  298.8 79.0 %psum.15 = f32[20,20]{0,1:T(8,128)S(1)} all-reduce(f32[20,20]{0,1:T(8,128)S(1)} %psum.14), channel_id=1, replica_groups=mesh['gx'=16,'gy'=8,'gz'=4] {'gx'}, use_global_device_ids=true, to_apply=%region_1.0 | all-reduce | flops 400 | bytes 3200 | tf_op jit(solution)/shard_map/psum | solution.py:95
  377.9 1.8 cholesky.19
  479.1 65.5 %subtract_divide_fusion = (f32[1,4]{1,0:T(1,128)S(1)}, f32[1,4]{1,0:T(1,128)S(1)}, f32[1,4]{1,0:T(1,128)S(1)}, f32[1,4]{1,0:T(1,128)S(1)}, f32[1,4]{1,0:T(1,128)...) fusion(f32[20,20]{1,0:T(8,128)S(1)} %multiply_select_fusion, ...), kind=kLoop, calls=%fused_computation.602 | loop fusion | flops 784 | bytes 884 | tf_op jit(solution)/shard_map/div | solution.py:62
  545.0 57.8 %fusion.191 = (f32[4]{0:T(128)S(1)}, f32[4]{0:T(128)S(1)}, f32[4]{0:T(128)S(1)}, f32[4]{0:T(128)S(1)}, f32[4]{0:T(128)S(1)}, /*index=5*/f32[4]{0:T(128)S(1)}, f3...) fusion(f32[20,20]{1,0:T(8,128)S(1)} %multiply_select_fusion, f32[1,4]{1,0:T(1,128)S(1)} %get-tuple-element.16, ...), kind=kLoop, calls=%fused_computation.504 | loop fusion | flops 704 | bytes 756 | tf_op jit(solution)/shard_map/div | solution.py:62
  602.8 19.3 %fusion.244 = (f32[1,4]{1,0:T(1,128)S(1)}, f32[4]{0:T(128)S(1)}) fusion(f32[1,4]{1,0:T(1,128)S(1)} %get-tuple-element.19, f32[1,4]{1,0:T(1,128)S(1)} %get-tuple-element.18, f32[1,4]{1,0:T(1,128)S(1)} %get-tuple-element.17, f32[1,4]{1,0:T(1,128)S(1)} %get-tuple-element.16, f32[4]{0:T(128)S(1)} %get-tuple-element.31, f32[4]{0:T(128)S(1)} %get-tuple-element.30, ...), kind=kLoop, calls=%fused_computation.656 | loop fusion | flops 240 | bytes 412 | tf_op jit(solution)/shard_map/stack | solution.py:63
  623.4 1.4 fusion
  (339 shorter events, 104.0 us)
Async XLA Ops:
  0.0 21.4 %copy-start.1 = (f32[4,5,32,128]{3,2,1,0:T(8,128)S(1)}, f32[4,5,32,128]{3,2,1,0:T(8,128)}, u32[]{:S(2)}) copy-start(f32[4,5,32,128]{3,2,1,0:T(8,128)} %param.3) | copy-start | bytes 983044
  0.9 28.4 %copy-start = (f32[4,5,32,128]{3,2,1,0:T(8,128)S(1)}, f32[4,5,32,128]{3,2,1,0:T(8,128)}, u32[]{:S(2)}) copy-start(f32[4,5,32,128]{3,2,1,0:T(8,128)} %param.5) | copy-start | bytes 983044
  0.9 15.5 %collective-permute-start.1 = (f32[4,1,32,128]{3,2,1,0:T(8,128)S(1)}, f32[4,1,32,128]{3,2,1,0:T(8,128)S(1)}, u32[]{:S(2)}, u32[]{:S(2)}) collective-permute-start(f32[4,1,32,128]{3,2,1,0:T(8,128)S(1)} %get-tuple-element.80), channel_id=1, source_target_pairs={{0,32},{32,64},{64,96},{96,128},{128,160},{160,192},{192,224},{224... | collective-permute-start | bytes 196616 | tf_op jit(solution)/shard_map/ppermute | solution.py:17
  6.5 11.0 %collective-permute-start.4 = (f32[4,1,32,128]{3,2,1,0:T(8,128)S(1)}, f32[4,1,32,128]{3,2,1,0:T(8,128)S(1)}, u32[]{:S(2)}, u32[]{:S(2)}) collective-permute-start(f32[4,1,32,128]{3,2,1,0:T(8,128)S(1)} %get-tuple-element.79), channel_id=1, source_target_pairs={{32,0},{64,32},{96,64},{128,96},{160,128},{192,160},{224,192},{256... | collective-permute-start | bytes 196616 | tf_op jit(solution)/shard_map/ppermute | solution.py:20
  12.1 9.3 %collective-permute-start.2 = (f32[4,1,32,128]{3,2,1,0:T(8,128)S(1)}, f32[4,1,32,128]{3,2,1,0:T(8,128)S(1)}, u32[]{:S(2)}, u32[]{:S(2)}) collective-permute-start(f32[4,1,32,128]{3,2,1,0:T(8,128)S(1)} %get-tuple-element.82), channel_id=1, source_target_pairs={{0,32},{32,64},{64,96},{96,128},{128,160},{160,192},{192,224},{224... | collective-permute-start | bytes 196616 | tf_op jit(solution)/shard_map/ppermute | solution.py:17
  14.0 7.5 %collective-permute-start = (f32[4,1,32,128]{3,2,1,0:T(8,128)S(1)}, f32[4,1,32,128]{3,2,1,0:T(8,128)S(1)}, u32[]{:S(2)}, u32[]{:S(2)}) collective-permute-start(f32[4,1,32,128]{3,2,1,0:T(8,128)S(1)} %get-tuple-element.81), channel_id=1, source_target_pairs={{32,0},{64,32},{96,64},{128,96},{160,128},{192,160},{224,192},{256... | collective-permute-start | bytes 196616 | tf_op jit(solution)/shard_map/ppermute | solution.py:20
  17.5 3.9 copy-start.20
  17.7 11.6 %copy-start.19 = (f32[4,7,32,128]{3,1,2,0:T(8,128)}, f32[4,7,32,128]{3,1,2,0:T(8,128)S(1)}, u32[]{:S(2)}) copy-start(f32[4,7,32,128]{3,1,2,0:T(8,128)S(1)} %copy.469) | copy-start | bytes 1376260
  18.4 12.8 %collective-permute-start.5 = (f32[4,7,1,128]{3,1,2,0:T(8,128)}, f32[4,7,1,128]{3,1,2,0:T(8,128)S(1)}, u32[]{:S(2)}, u32[]{:S(2)}) collective-permute-start(f32[4,7,1,128]{3,1,2,0:T(8,128)} %get-tuple-element.50), channel_id=1, source_target_pairs={{0,4},{4,8},{8,12},{12,16},{16,20},{20,24},{24,28},{1,5},{5,9},{9,... | collective-permute-start | bytes 43016 | tf_op jit(solution)/shard_map/ppermute | solution.py:17
  20.1 13.1 %collective-permute-start.8 = (f32[4,7,1,128]{3,1,2,0:T(8,128)}, f32[4,7,1,128]{3,1,2,0:T(8,128)S(1)}, u32[]{:S(2)}, u32[]{:S(2)}) collective-permute-start(f32[4,7,1,128]{3,1,2,0:T(8,128)} %get-tuple-element.51), channel_id=1, source_target_pairs={{4,0},{8,4},{12,8},{16,12},{20,16},{24,20},{28,24},{5,1},{9,5},{13... | collective-permute-start | bytes 43016 | tf_op jit(solution)/shard_map/ppermute | solution.py:20
  21.5 2.7 copy-start.24
  21.5 2.6 copy-start.17
  22.2 16.9 %collective-permute-start.3 = (f32[4,7,1,128]{3,0,2,1:T(4,128)}, f32[4,7,1,128]{3,0,2,1:T(4,128)}, u32[]{:S(2)}, u32[]{:S(2)}) collective-permute-start(f32[4,7,1,128]{3,0,2,1:T(4,128)} %copy.550), channel_id=1, source_target_pairs={{4,0},{8,4},{12,8},{16,12},{20,16},{24,20},{28,24},{5,1},{9,5},{13... | collective-permute-start | bytes 43016 | tf_op jit(solution)/shard_map/ppermute | solution.py:20
  24.1 15.8 %collective-permute-start.6 = (f32[4,7,1,128]{3,0,2,1:T(4,128)}, f32[4,7,1,128]{3,0,2,1:T(4,128)}, u32[]{:S(2)}, u32[]{:S(2)}) collective-permute-start(f32[4,7,1,128]{3,0,2,1:T(4,128)} %copy.551), channel_id=1, source_target_pairs={{0,4},{4,8},{8,12},{12,16},{16,20},{20,24},{24,28},{1,5},{5,9},{9,... | collective-permute-start | bytes 43016 | tf_op jit(solution)/shard_map/ppermute | solution.py:17
  29.4 55.7 %copy-start.5 = (f32[5,32,128]{2,1,0:T(8,128)}, f32[5,32,128]{2,1,0:T(8,128)S(1)}, u32[]{:S(2)}) copy-start(f32[5,32,128]{2,1,0:T(8,128)S(1)} %get-tuple-element.77) | copy-start | bytes 245764
  29.4 55.7 %copy-start.8 = (f32[5,32,128]{2,1,0:T(8,128)}, f32[5,32,128]{2,1,0:T(8,128)S(1)}, u32[]{:S(2)}) copy-start(f32[5,32,128]{2,1,0:T(8,128)S(1)} %get-tuple-element.78) | copy-start | bytes 245764
  29.4 109.4 %copy-start.3 = (f32[5,32,128]{2,1,0:T(8,128)}, f32[5,32,128]{2,1,0:T(8,128)S(1)}, u32[]{:S(2)}) copy-start(f32[5,32,128]{2,1,0:T(8,128)S(1)} %get-tuple-element.76) | copy-start | bytes 245764
  35.2 5.5 copy-start.18
  36.0 14.8 %collective-permute-start.9 = (f32[4,7,34,1]{2,1,3,0:T(8,128)S(1)}, f32[4,7,34,1]{2,1,3,0:T(8,128)S(1)}, u32[]{:S(2)}, u32[]{:S(2)}) collective-permute-start(f32[4,7,34,1]{2,1,3,0:T(8,128)S(1)} %pad_maximum_fusion.93), channel_id=1, source_target_pairs={{0,1},{1,2},{2,3},{4,5},{5,6},{6,7},{8,9},{9,10},{10,11},{12,13},{... | collective-permute-start | bytes 11432 | tf_op jit(solution)/shard_map/ppermute | solution.py:17
  43.2 11.2 %collective-permute-start.7 = (f32[4,7,34,1]{2,0,3,1:T(4,128)S(1)}, f32[4,7,34,1]{2,0,3,1:T(4,128)S(1)}, u32[]{:S(2)}, u32[]{:S(2)}) collective-permute-start(f32[4,7,34,1]{2,0,3,1:T(4,128)S(1)} %copy.476), channel_id=1, source_target_pairs={{1,0},{2,1},{3,2},{5,4},{6,5},{7,6},{9,8},{10,9},{11,10},{13,12},{... | collective-permute-start | bytes 11432 | tf_op jit(solution)/shard_map/ppermute | solution.py:20
  45.9 9.7 %collective-permute-start.10 = (f32[4,7,34,1]{2,0,3,1:T(4,128)S(1)}, f32[4,7,34,1]{2,0,3,1:T(4,128)S(1)}, u32[]{:S(2)}, u32[]{:S(2)}) collective-permute-start(f32[4,7,34,1]{2,0,3,1:T(4,128)S(1)} %copy.483), channel_id=1, source_target_pairs={{0,1},{1,2},{2,3},{4,5},{5,6},{6,7},{8,9},{9,10},{10,11},{12,13},{... | collective-permute-start | bytes 11432 | tf_op jit(solution)/shard_map/ppermute | solution.py:17
  50.8 34.3 %copy-start.11 = (f32[5,32,128]{2,1,0:T(8,128)}, f32[5,32,128]{2,1,0:T(8,128)S(1)}, u32[]{:S(2)}) copy-start(f32[5,32,128]{2,1,0:T(8,128)S(1)} %copy.471) | copy-start | bytes 245764
  53.2 3.5 copy-start.23
  53.2 3.5 copy-start.25
  54.4 84.4 %copy-start.14 = (f32[5,32,128]{2,1,0:T(8,128)}, f32[5,32,128]{2,1,0:T(8,128)S(1)}, u32[]{:S(2)}) copy-start(f32[5,32,128]{2,1,0:T(8,128)S(1)} %copy.482) | copy-start | bytes 245764
  58.9 7.3 %collective-permute-start.11 = (f32[4,1,32,128]{3,2,1,0:T(8,128)S(1)}, f32[4,1,32,128]{3,2,1,0:T(8,128)S(1)}, u32[]{:S(2)}, u32[]{:S(2)}) collective-permute-start(f32[4,1,32,128]{3,2,1,0:T(8,128)S(1)} %get-tuple-element.73), channel_id=1, source_target_pairs={{32,0},{64,32},{96,64},{128,96},{160,128},{192,160},{224,192},{256... | collective-permute-start | bytes 196616 | tf_op jit(solution)/shard_map/ppermute | solution.py:20
  60.8 6.6 %collective-permute-start.12 = (f32[4,1,32,128]{3,2,1,0:T(8,128)S(1)}, f32[4,1,32,128]{3,2,1,0:T(8,128)S(1)}, u32[]{:S(2)}, u32[]{:S(2)}) collective-permute-start(f32[4,1,32,128]{3,2,1,0:T(8,128)S(1)} %get-tuple-element.72), channel_id=1, source_target_pairs={{0,32},{32,64},{64,96},{96,128},{128,160},{160,192},{192,224},{224... | collective-permute-start | bytes 196616 | tf_op jit(solution)/shard_map/ppermute | solution.py:17
  67.5 5.3 collective-permute-start.13
  68.8 4.8 collective-permute-start.14
  76.2 6.6 %collective-permute-start.15 = (f32[4,7,34,1]{2,0,3,1:T(4,128)S(1)}, f32[4,7,34,1]{2,0,3,1:T(4,128)S(1)}, u32[]{:S(2)}, u32[]{:S(2)}) collective-permute-start(f32[4,7,34,1]{2,0,3,1:T(4,128)S(1)} %copy.491), channel_id=1, source_target_pairs={{1,0},{2,1},{3,2},{5,4},{6,5},{7,6},{9,8},{10,9},{11,10},{13,12},{... | collective-permute-start | bytes 11432 | tf_op jit(solution)/shard_map/ppermute | solution.py:20
  78.9 5.1 collective-permute-start.16
  86.8 1.2 copy-start.16
  88.8 8.2 %collective-permute-start.17 = (f32[4,1,32,128]{3,2,1,0:T(8,128)S(1)}, f32[4,1,32,128]{3,2,1,0:T(8,128)S(1)}, u32[]{:S(2)}, u32[]{:S(2)}) collective-permute-start(f32[4,1,32,128]{3,2,1,0:T(8,128)S(1)} %get-tuple-element.71), channel_id=1, source_target_pairs={{32,0},{64,32},{96,64},{128,96},{160,128},{192,160},{224,192},{256... | collective-permute-start | bytes 196616 | tf_op jit(solution)/shard_map/ppermute | solution.py:20
  90.7 7.5 %collective-permute-start.18 = (f32[4,1,32,128]{3,2,1,0:T(8,128)S(1)}, f32[4,1,32,128]{3,2,1,0:T(8,128)S(1)}, u32[]{:S(2)}, u32[]{:S(2)}) collective-permute-start(f32[4,1,32,128]{3,2,1,0:T(8,128)S(1)} %get-tuple-element.70), channel_id=1, source_target_pairs={{0,32},{32,64},{64,96},{96,128},{128,160},{160,192},{192,224},{224... | collective-permute-start | bytes 196616 | tf_op jit(solution)/shard_map/ppermute | solution.py:17
  98.3 5.9 collective-permute-start.19
  99.6 5.4 collective-permute-start.20
  105.3 8.0 %copy-start.6 = (f32[5,32,128]{2,1,0:T(8,128)S(1)}, f32[5,32,128]{2,1,0:T(8,128)}, u32[]{:S(2)}) copy-start(f32[5,32,128]{2,1,0:T(8,128)} %copy-done.5) | copy-start | bytes 245764
  105.3 8.0 %copy-start.9 = (f32[5,32,128]{2,1,0:T(8,128)S(1)}, f32[5,32,128]{2,1,0:T(8,128)}, u32[]{:S(2)}) copy-start(f32[5,32,128]{2,1,0:T(8,128)} %copy-done.8) | copy-start | bytes 245764
  105.3 8.0 %copy-start.12 = (f32[5,32,128]{2,1,0:T(8,128)S(1)}, f32[5,32,128]{2,1,0:T(8,128)}, u32[]{:S(2)}) copy-start(f32[5,32,128]{2,1,0:T(8,128)} %copy-done.11) | copy-start | bytes 245764
  105.6 7.0 %collective-permute-start.21 = (f32[4,7,34,1]{2,0,3,1:T(4,128)S(1)}, f32[4,7,34,1]{2,0,3,1:T(4,128)S(1)}, u32[]{:S(2)}, u32[]{:S(2)}) collective-permute-start(f32[4,7,34,1]{2,0,3,1:T(4,128)S(1)} %copy.501), channel_id=1, source_target_pairs={{1,0},{2,1},{3,2},{5,4},{6,5},{7,6},{9,8},{10,9},{11,10},{13,12},{... | collective-permute-start | bytes 11432 | tf_op jit(solution)/shard_map/ppermute | solution.py:20
  107.2 5.8 collective-permute-start.22
  112.6 26.2 %copy-start.21 = (f32[5,32,128]{2,1,0:T(8,128)}, f32[5,32,128]{2,1,0:T(8,128)S(1)}, u32[]{:S(2)}) copy-start(f32[5,32,128]{2,1,0:T(8,128)S(1)} %broadcast_multiply_fusion.3) | copy-start | bytes 245764
  115.3 7.5 %collective-permute-start.23 = (f32[4,1,32,128]{3,2,1,0:T(8,128)S(1)}, f32[4,1,32,128]{3,2,1,0:T(8,128)S(1)}, u32[]{:S(2)}, u32[]{:S(2)}) collective-permute-start(f32[4,1,32,128]{3,2,1,0:T(8,128)S(1)} %get-tuple-element.69), channel_id=1, source_target_pairs={{32,0},{64,32},{96,64},{128,96},{160,128},{192,160},{224,192},{256... | collective-permute-start | bytes 196616 | tf_op jit(solution)/shard_map/ppermute | solution.py:20
  117.3 6.9 %collective-permute-start.24 = (f32[4,1,32,128]{3,2,1,0:T(8,128)S(1)}, f32[4,1,32,128]{3,2,1,0:T(8,128)S(1)}, u32[]{:S(2)}, u32[]{:S(2)}) collective-permute-start(f32[4,1,32,128]{3,2,1,0:T(8,128)S(1)} %get-tuple-element.68), channel_id=1, source_target_pairs={{0,32},{32,64},{64,96},{96,128},{128,160},{160,192},{192,224},{224... | collective-permute-start | bytes 196616 | tf_op jit(solution)/shard_map/ppermute | solution.py:17
  124.2 5.9 collective-permute-start.25
  125.5 5.4 collective-permute-start.26
  131.5 6.1 collective-permute-start.27
  133.1 5.4 collective-permute-start.28
  139.3 7.9 %collective-permute-start.29 = (f32[4,1,32,128]{3,2,1,0:T(8,128)S(1)}, f32[4,1,32,128]{3,2,1,0:T(8,128)S(1)}, u32[]{:S(2)}, u32[]{:S(2)}) collective-permute-start(f32[4,1,32,128]{3,2,1,0:T(8,128)S(1)} %get-tuple-element.63), channel_id=1, source_target_pairs={{32,0},{64,32},{96,64},{128,96},{160,128},{192,160},{224,192},{256... | collective-permute-start | bytes 196616 | tf_op jit(solution)/shard_map/ppermute | solution.py:20
  141.2 7.3 %collective-permute-start.30 = (f32[4,1,32,128]{3,2,1,0:T(8,128)S(1)}, f32[4,1,32,128]{3,2,1,0:T(8,128)S(1)}, u32[]{:S(2)}, u32[]{:S(2)}) collective-permute-start(f32[4,1,32,128]{3,2,1,0:T(8,128)S(1)} %get-tuple-element.62), channel_id=1, source_target_pairs={{0,32},{32,64},{64,96},{96,128},{128,160},{160,192},{192,224},{224... | collective-permute-start | bytes 196616 | tf_op jit(solution)/shard_map/ppermute | solution.py:17
  148.6 7.5 %collective-permute-start.31 = (f32[4,7,1,128]{3,0,2,1:T(4,128)S(1)}, f32[4,7,1,128]{3,0,2,1:T(4,128)S(1)}, u32[]{:S(2)}, u32[]{:S(2)}) collective-permute-start(f32[4,7,1,128]{3,0,2,1:T(4,128)S(1)} %copy.515), channel_id=1, source_target_pairs={{4,0},{8,4},{12,8},{16,12},{20,16},{24,20},{28,24},{5,1},{9,5},{13... | collective-permute-start | bytes 43016 | tf_op jit(solution)/shard_map/ppermute | solution.py:20
  149.9 6.3 %collective-permute-start.32 = (f32[4,7,1,128]{3,0,2,1:T(4,128)S(1)}, f32[4,7,1,128]{3,0,2,1:T(4,128)S(1)}, u32[]{:S(2)}, u32[]{:S(2)}) collective-permute-start(f32[4,7,1,128]{3,0,2,1:T(4,128)S(1)} %copy.517), channel_id=1, source_target_pairs={{0,4},{4,8},{8,12},{12,16},{16,20},{20,24},{24,28},{1,5},{5,9},{9,... | collective-permute-start | bytes 43016 | tf_op jit(solution)/shard_map/ppermute | solution.py:17
  156.8 11.5 %collective-permute-start.33 = (f32[4,7,34,1]{2,0,3,1:T(4,128)S(1)}, f32[4,7,34,1]{2,0,3,1:T(4,128)}, u32[]{:S(2)}, u32[]{:S(2)}) collective-permute-start(f32[4,7,34,1]{2,0,3,1:T(4,128)S(1)} %copy.521), channel_id=1, source_target_pairs={{1,0},{2,1},{3,2},{5,4},{6,5},{7,6},{9,8},{10,9},{11,10},{13,12},{... | collective-permute-start | bytes 11432 | tf_op jit(solution)/shard_map/ppermute | solution.py:20
  159.0 10.4 %collective-permute-start.34 = (f32[4,7,34,1]{2,0,3,1:T(4,128)}, f32[4,7,34,1]{2,0,3,1:T(4,128)}, u32[]{:S(2)}, u32[]{:S(2)}) collective-permute-start(f32[4,7,34,1]{2,0,3,1:T(4,128)} %copy.523), channel_id=1, source_target_pairs={{0,1},{1,2},{2,3},{4,5},{5,6},{6,7},{8,9},{9,10},{10,11},{12,13},{... | collective-permute-start | bytes 11432 | tf_op jit(solution)/shard_map/ppermute | solution.py:17
  166.6 4.5 copy-start.4
  166.6 4.6 copy-start.7
  166.6 4.6 copy-start.10
  166.6 4.6 copy-start.13
  166.6 4.6 copy-start.15
  166.6 4.6 copy-start.22
  468.5 156.3 %copy-start.2 = (f32[4,5,32,128]{3,2,1,0:T(8,128)S(1)}, f32[4,5,32,128]{3,2,1,0:T(8,128)}, u32[]{:S(2)}) copy-start(f32[4,5,32,128]{3,2,1,0:T(8,128)} %param.3) | copy-start | bytes 983044
